TPU v7x, 256 devices: a whole 4x4x8 slice. The times are simulated.
256 devices in a mesh: front: 64 (over x, y, z_lo, core), blk: 4 (over z_hi).
Axes of the slice: x: 4, y: 4, z: 8 (z_hi: 4, z_lo: 2; z = z_hi * 2 + z_lo), core: 2. Of those that a mesh axis runs over, the one named last changes fastest.
Arguments:
- child_diag: float32 [65536, 1024], P(('front', 'blk')), as said below
- child_top: float32 [32768, 1024], P(('front', 'blk')), may hold values from -0.078125 to 0.078125
- child_rows: float32 [131072, 1024], P(('front', 'blk')), may hold values from -12 to 12
- row_owner: int32 [64, 16, 1], P('front'), may hold values from 0 to 63; in each aligned block of 16 rows (0 to 15, 16 to 31, ..., all dimensions but the last counted through in order) at most 2 rows name the same one
- row_slot: int32 [64, 16], P('front'), may hold values from 0 to 3
- col_block: int32 [64, 4], P('front'), may hold values from 0 to 1
- parent_diag: float32 [1024, 1024], P('blk'), as said below
- parent_rows: float32 [32768, 1024], P('front', 'blk'), may hold values from -6 to 6
Outputs:
- parent_factor: float32 [1024, 1024], P('blk')
- parent_panel: float32 [32768, 1024], P(('front', 'blk'))
Inputs may be any that keep to these rules, and one draw needn't show every extreme that they name: `row_owner`: within the 16 row blocks of one child no owner is named more than 2 times, and in some children one owner is named exactly 2 times. `child_diag`: each 1024 x 1024 block is symmetric with all eigenvalues at least 1. `parent_diag`: symmetric with all eigenvalues at least 24; parent_diag - diag_update has all eigenvalues at least 12.
All inputs are finite; a program needn't handle non-finite values.
Results may differ from a plain program's by a relative error of at most 0.0001.
Values sent between devices are 32-bit elements; how exact they have to be, the bound alone decides.
A program may use at most 192 MiB of HBM per device.

v0:
```python
import jax
import jax.numpy as jnp
from jax import lax
from jax.sharding import PartitionSpec as P

W = 1024
TILE = 128
TA = 4
PB = 4


HIGHEST = lax.Precision.HIGHEST


def right_solve(factor, matrix):
    return jax.scipy.linalg.solve_triangular(factor, matrix.T, lower=True).T


def blocked_cholesky(matrix):
    order_size = matrix.shape[0]
    stride = min(256, order_size)
    remaining = matrix
    factor = jnp.zeros_like(matrix)
    for offset in range(0, order_size, stride):
        finish = offset + stride
        diag_piece = jnp.linalg.cholesky(remaining[offset:finish, offset:finish])
        factor = factor.at[offset:finish, offset:finish].set(diag_piece)
        if finish < order_size:
            lower_part = right_solve(diag_piece, remaining[finish:, offset:finish])
            factor = factor.at[finish:, offset:finish].set(lower_part)
            trailing = remaining[finish:, finish:] - jnp.dot(
                lower_part, lower_part.T, precision=HIGHEST
            )
            remaining = remaining.at[finish:, finish:].set(trailing)
    return factor


def shards(
    child_diag, child_top, child_rows, row_owner, row_slot, col_block, parent_diag, parent_rows
):
    block_count = lax.axis_size("blk")
    front_count = lax.axis_size("front")
    my_block = lax.axis_index("blk")
    quarter = W // (TILE * block_count)
    block_width = W // TILE
    capacity = max(2, 8 * TA // front_count)
    diag_whole, top_whole = (
        lax.all_gather(child_diag, "blk", axis=0, tiled=True),
        lax.all_gather(child_top, "blk", axis=0, tiled=True),
    )
    factor = blocked_cholesky(diag_whole)
    top_solved = right_solve(factor, top_whole)
    rows_solved = right_solve(factor, child_rows)
    top_tiles = top_solved.reshape(block_count, TILE, W)
    schur_tiles = jnp.einsum("rw,kcw->krc", rows_solved, top_tiles, precision=HIGHEST)
    arrived = lax.all_to_all(schur_tiles, "blk", split_axis=0, concat_axis=0, tiled=True)
    arrived = arrived.reshape(block_count * TA, TILE, TILE)
    owners = row_owner[0, :, 0]
    slot_index = row_slot[0]
    column_picks = col_block[0]
    sequence = jnp.arange(owners.shape[0], dtype=jnp.int32)
    earlier = (owners[:, None] == owners[None, :]) & (sequence[None, :] < sequence[:, None])
    arrival_rank = jnp.sum(earlier.astype(jnp.int32), axis=1)
    position = owners * capacity + arrival_rank
    block_ids = jnp.arange(block_count, dtype=jnp.int32)
    my_pick = jnp.sum(jnp.where(block_ids == my_block, column_picks, 0))
    landing = slot_index * quarter + my_pick
    outgoing = (
        jnp.zeros((front_count * capacity, TILE, TILE), jnp.float32).at[position].set(arrived)
    )
    labels = jnp.zeros((front_count * capacity,), jnp.int32).at[position].set(landing)
    received, received_labels = (
        lax.all_to_all(
            outgoing.reshape(front_count, capacity, TILE, TILE),
            "front",
            split_axis=0,
            concat_axis=0,
            tiled=True,
        ),
        lax.all_to_all(
            labels.reshape(front_count, capacity), "front", split_axis=0, concat_axis=0, tiled=True
        ),
    )
    tile_sums = (
        jnp.zeros((PB * quarter, TILE, TILE), jnp.float32)
        .at[received_labels.reshape(-1)]
        .add(received.reshape(-1, TILE, TILE))
    )
    panel_update = (
        tile_sums.reshape(PB, quarter, TILE, TILE)
        .transpose(0, 2, 1, 3)
        .reshape(PB * TILE, quarter * TILE)
    )
    updated = parent_rows - panel_update
    row_major = lax.all_to_all(updated, "blk", split_axis=0, concat_axis=1, tiled=True)
    columns = block_ids * quarter + column_picks
    my_top = lax.dynamic_slice_in_dim(top_solved, my_block * TILE, TILE, 0)
    cross_terms = jnp.dot(my_top, top_solved.T, precision=HIGHEST)
    cross_terms = cross_terms.reshape(TILE, block_count, TILE).transpose(1, 0, 2)
    row_block = my_block * quarter + my_pick
    spread = (
        jnp.zeros((block_width, TILE, block_width, TILE), jnp.float32)
        .at[row_block, :, columns, :]
        .set(cross_terms)
    )
    owner_mask = jnp.where(lax.axis_index("front") == 0, 1.0, 0.0).astype(jnp.float32)
    placed = lax.dynamic_update_slice_in_dim(
        jnp.zeros((W, W), jnp.float32), parent_diag * owner_mask, my_block * quarter * TILE, 0
    )
    whole_diag = lax.psum(placed - spread.reshape(W, W), ("front", "blk"))
    parent_factor = blocked_cholesky(whole_diag)
    own_rows = lax.dynamic_slice_in_dim(parent_factor, my_block * quarter * TILE, quarter * TILE, 0)
    return (own_rows, right_solve(parent_factor, row_major))


def solution(mesh):
    return jax.shard_map(
        shards,
        mesh=mesh,
        in_specs=(
            P(("front", "blk"), None),
            P(("front", "blk"), None),
            P(("front", "blk"), None),
            P("front", None, None),
            P("front", None),
            P("front", None),
            P("blk", None),
            P("front", "blk"),
        ),
        out_specs=(P("blk", None), P(("front", "blk"), None)),
        check_vma=False,
    )
```

profile of v0, /device:TPU:2, one launch (start us, length us, event | category | flops | bytes accessed | tf_op | source)
XLA Modules:
  0.0 1292.3 jit_solution(12158726002848538924)
XLA Ops:
  7.2 2.7 copy.197
  12.9 81.6 %all-gather.3.cloned.1.call-done = f32[1024,1024]{0,1:T(8,128)} async-done(((f32[256,1024]{0,1:T(8,128)}), f32[1024,1024]{0,1:T(8,128)}) %all-gather.3.cloned.1.call-update) | async-done | bytes 4194320 | tf_op jit(solution)/shard_map/all_gather | solution.py:48
  96.6 11.7 cholesky.382
  108.4 9.8 custom-call.38
  118.7 11.7 cholesky.399
  132.5 3.9 while.38
  136.4 20.1 %custom-call.39 = f32[2,128,128]{1,2,0:T(8,128)S(1)} custom-call(f32[2,128,128]{2,1,0:T(8,128)S(1)} %get-tuple-element.311), custom_call_target="InvertDiagBlocksLowerTriangular" | custom-call | tf_op jit(solution)/shard_map/jit(_solve_triangular)/triangular_solve | solution.py:16
  159.7 3.8 slice_subtract_fusion.1
  164.4 2.5 scatter.66
  169.0 11.7 cholesky.416
  180.8 10.4 custom-call.40
  192.5 11.9 cholesky.433
  207.9 4.1 while.39
  212.0 19.7 %custom-call.41 = f32[2,128,128]{1,2,0:T(8,128)S(1)} custom-call(f32[2,128,128]{2,1,0:T(8,128)S(1)} %get-tuple-element.312), custom_call_target="InvertDiagBlocksLowerTriangular" | custom-call | tf_op jit(solution)/shard_map/jit(_solve_triangular)/triangular_solve | solution.py:16
  238.9 11.7 cholesky.450
  250.6 9.8 custom-call.42
  260.9 11.7 cholesky.467
  276.1 4.1 while.40
  280.3 20.1 %custom-call.43 = f32[2,128,128]{1,2,0:T(8,128)S(1)} custom-call(f32[2,128,128]{2,1,0:T(8,128)S(1)} %get-tuple-element.313), custom_call_target="InvertDiagBlocksLowerTriangular" | custom-call | tf_op jit(solution)/shard_map/jit(_solve_triangular)/triangular_solve | solution.py:16
  302.0 11.7 cholesky.484
  313.8 9.8 custom-call.44
  324.1 11.7 cholesky.501
  340.1 4.8 fusion.1
  344.9 23.0 %while.41 = (s32[]{:T(128)}, f32[1024,1024]{1,0:T(8,128)}, s32[8,2]{0,1:T(2,128)S(1)}, f32[8,128,128]{2,1,0:T(8,128)S(1)}, s32[]{:T(128)}) while((s32[]{:T(128)}, f32[1024,1024]{1,0:T(8,128)}, s32[8,2]{0,1:T(2,128)S(1)}, f32[8,128,128]{2,1,0:T(8,128)S(1)}, s32[]{:T(128)}) %tuple.338), condition=%wide.while_cond.23, body=%wide.while_body.23.sunk | while | flops 2 | bytes 131181 | solution.py:16
  367.9 78.8 %custom-call.45 = f32[8,128,128]{1,2,0:T(8,128)S(1)} custom-call(f32[8,128,128]{2,1,0:T(8,128)S(1)} %get-tuple-element.314), custom_call_target="InvertDiagBlocksLowerTriangular" | custom-call | tf_op jit(solution)/shard_map/jit(_solve_triangular)/triangular_solve | solution.py:16
  487.1 6.7 fusion.4
  493.8 9.4 all-to-all-start.1
  506.8 2.5 copy.196
  509.3 2.5 broadcast.498
  512.9 16.0 %all-to-all-done.1 = f32[4,512,128]{1,2,0:T(8,128)S(1)} async-done(((f32[4,512,128]{1,2,0:T(8,128)}), f32[4,512,128]{1,2,0:T(8,128)S(1)}, u32[]{:S(2)}, u32[]{:S(2)}) %all-to-all-start.1) | async-done | bytes 1048608 | tf_op jit(solution)/shard_map/all_to_all | solution.py:56
  528.9 10.3 all-to-all-start
  540.6 4.3 broadcast_in_dim.27
  544.9 3.0 scatter_fusion.1
  547.9 9.1 all-to-all-start.2
  558.4 2.5 broadcast_in_dim.13
  563.1 5.5 copy.213
  568.7 7.0 bitcast_subtract_fusion
  577.0 314.4 %all-reduce.6.cloned.1.call-done = f32[1024,1024]{0,1:T(8,128)} async-done(((f32[1024,1024]{0,1:T(8,128)}), f32[1024,1024]{0,1:T(8,128)}) %all-reduce.6.cloned.1.call-update) | async-done | bytes 4194320 | tf_op jit(solution)/shard_map/psum | solution.py:110
  893.5 11.7 cholesky.518
  905.4 9.8 custom-call.46
  915.8 11.7 cholesky.535
  931.4 4.1 while.42
  935.5 19.7 %custom-call.47 = f32[2,128,128]{1,2,0:T(8,128)S(1)} custom-call(f32[2,128,128]{2,1,0:T(8,128)S(1)} %get-tuple-element.315), custom_call_target="InvertDiagBlocksLowerTriangular" | custom-call | tf_op jit(solution)/shard_map/jit(_solve_triangular)/triangular_solve | solution.py:16
  963.0 11.7 cholesky.552
  974.8 9.8 custom-call.48
  986.9 11.9 cholesky.569
  998.9 3.5 scatter.80
  1006.7 4.2 while.43
  1011.0 19.7 %custom-call.49 = f32[2,128,128]{1,2,0:T(8,128)S(1)} custom-call(f32[2,128,128]{2,1,0:T(8,128)S(1)} %get-tuple-element.316), custom_call_target="InvertDiagBlocksLowerTriangular" | custom-call | tf_op jit(solution)/shard_map/jit(_solve_triangular)/triangular_solve | solution.py:16
  1033.4 11.7 cholesky.586
  1045.2 9.8 custom-call.50
  1055.6 12.1 cholesky.603
  1072.2 4.2 while.44
  1076.5 19.7 %custom-call.51 = f32[2,128,128]{1,2,0:T(8,128)S(1)} custom-call(f32[2,128,128]{2,1,0:T(8,128)S(1)} %get-tuple-element.317), custom_call_target="InvertDiagBlocksLowerTriangular" | custom-call | tf_op jit(solution)/shard_map/jit(_solve_triangular)/triangular_solve | solution.py:16
  1097.9 11.7 cholesky.620
  1109.7 9.8 custom-call.52
  1120.1 11.7 cholesky.637
  1136.1 4.7 fusion
  1140.9 17.2 %scatter_fusion.2 = f32[8,128,128]{2,1,0:T(8,128)S(1)} fusion(f32[8,128,128]{2,1,0:T(8,128)S(1)} %broadcast.606.clone.1, s32[128]{0:T(128)S(1)} %fusion.185, f32[128,128,128]{2,1,0:T(8,128)} %bitcast.84), kind=kCustom, calls=%fused_computation.3 | custom fusion | flops 2097152 | bytes 25166336 | tf_op jit(solution)/shard_map/scatter-add | solution.py:87
  1159.4 5.6 all-to-all-start.3
  1165.0 25.1 %while.37 = (s32[]{:T(128)}, f32[1024,1024]{0,1:T(8,128)}, s32[8,2]{0,1:T(2,128)S(1)}, f32[8,128,128]{2,1,0:T(8,128)S(1)}, s32[]{:T(128)}) while((s32[]{:T(128)}, f32[1024,1024]{0,1:T(8,128)}, s32[8,2]{0,1:T(2,128)S(1)}, f32[8,128,128]{2,1,0:T(8,128)S(1)}, s32[]{:T(128)}) %tuple.359), condition=%wide.while_cond.24, body=%wide.while_body.24.sunk | while | flops 2 | bytes 393321 | solution.py:16
  1178.2 2.3 dynamic-slice.207
  1181.4 2.3 dynamic-slice.207
  1190.0 78.6 %custom-call.24 = f32[8,128,128]{1,2,0:T(8,128)S(1)} custom-call(f32[8,128,128]{2,1,0:T(8,128)S(1)} %get-tuple-element.286), custom_call_target="InvertDiagBlocksLowerTriangular" | custom-call | tf_op jit(solution)/shard_map/jit(_solve_triangular)/triangular_solve | solution.py:16
  (386 shorter events, 197.2 us)
Async XLA Ops:
  7.2 2.8 copy-start.13
  7.2 3.9 copy-start.9
  7.2 87.3 %all-gather.3.cloned.1.call-start = ((), (), s32[]{:S(2)}) async-start(), calls=%async_computation.4 | async-start | bytes 5242880 | tf_op jit(solution)/shard_map/all_gather | solution.py:48
  9.9 456.9 %all-gather.5.cloned.1.call-start = ((), (), s32[]{:S(2)}) async-start(), calls=%async_computation.5 | async-start | bytes 2621440 | tf_op jit(solution)/shard_map/all_gather | solution.py:49
  234.1 3.7 copy-start.8
  340.1 106.7 %copy-start = (f32[512,1024]{0,1:T(8,128)S(1)}, f32[512,1024]{0,1:T(8,128)}, u32[]{:S(2)}) copy-start(f32[512,1024]{0,1:T(8,128)} %copy.238) | copy-start | bytes 6291460
  466.8 3.4 copy-start.10
  493.8 9.4 copy-start.14
  493.8 10.7 copy-start.16
  493.8 10.9 copy-start.15
  493.8 35.1 %all-to-all-start.1 = ((f32[4,512,128]{1,2,0:T(8,128)}), f32[4,512,128]{1,2,0:T(8,128)S(1)}, u32[]{:S(2)}, u32[]{:S(2)}) async-start(f32[4,512,128]{1,2,0:T(8,128)} %fusion.4), calls=%async_computation.1 | async-start | bytes 2097152 | tf_op jit(solution)/shard_map/all_to_all | solution.py:56
  509.3 2.5 copy-start.4
  528.9 18.9 %all-to-all-start = ((s32[64,1,2]{2,1,0:T(1,128)}), s32[64,1,2]{2,1,0:T(1,128)S(1)}, u32[]{:S(2)}, u32[]{:S(2)}) async-start(s32[64,1,2]{2,1,0:T(1,128)} %bitcast.67), calls=%async_computation | async-start | bytes 65536 | tf_op jit(solution)/shard_map/all_to_all | solution.py:80
  540.6 4.3 copy-start.1
  547.9 593.0 %all-to-all-start.2 = ((f32[64,2,128,128]{3,2,1,0:T(8,128)}), f32[64,2,128,128]{3,2,1,0:T(8,128)}, u32[]{:S(2)}, u32[]{:S(2)}) async-start(f32[64,2,128,128]{3,2,1,0:T(8,128)} %bitcast.457), calls=%async_computation.2 | async-start | bytes 16777216 | tf_op jit(solution)/shard_map/all_to_all | solution.py:73
  557.0 334.5 %all-reduce.6.cloned.1.call-start = ((), (), s32[]{:S(2)}) async-start(), calls=%async_computation.6 | async-start | bytes 8388608 | tf_op jit(solution)/shard_map/psum | solution.py:110
  955.2 2.9 copy-start.5
  962.2 0.7 copy-start.11
  1031.1 2.0 copy-start.2
  1032.0 1.1 copy-start.6
  1033.1 37.4 %copy-start.3 = (f32[128,512]{1,0:T(8,128)S(1)}, f32[128,512]{1,0:T(8,128)}, u32[]{:S(2)}) copy-start(f32[128,512]{1,0:T(8,128)} %copy-done.2) | copy-start | bytes 786436
  1033.2 37.4 %copy-start.7 = (f32[128,512]{1,0:T(8,128)S(1)}, f32[128,512]{1,0:T(8,128)}, u32[]{:S(2)}) copy-start(f32[128,512]{1,0:T(8,128)} %copy-done.6) | copy-start | bytes 786436
  1140.9 17.6 %copy-start.12 = (f32[512,256]{1,0:T(8,128)S(1)}, f32[512,256]{1,0:T(8,128)}, u32[]{:S(2)}) copy-start(f32[512,256]{1,0:T(8,128)} %param.64) | copy-start | bytes 1572868
  1159.4 111.9 %all-to-all-start.3 = ((f32[4,128,256]{2,1,0:T(8,128)}), f32[4,128,256]{2,1,0:T(8,128)S(1)}, u32[]{:S(2)}, u32[]{:S(2)}) async-start(f32[4,128,256]{2,1,0:T(8,128)} %bitcast.87), calls=%async_computation.3 | async-start | bytes 1048576 | tf_op jit(solution)/shard_map/all_to_all | solution.py:95
Sparse Core Ops, SparseCore 0:
  10.4 84.0 all-gather.2
  96.9 59.9 all-gather.4
  575.8 315.6 all-reduce.5
where the time goes:
time: 1300 us; the launch traced here: 1290 us
  other arithmetic  605 us (47%)
  waiting for transfers between devices  412 us (32%)
  local copies, waits for them, and re-layouts  128 us (10%)
  matrix products  85.6 us (7%)
  starting transfers between devices  34.5 us (3%)
  between operations  26.6 us (2%)
    psum x1, waiting for transfers between devices, shards(): whole_diag = lax.psum(placed - spread.reshape(W, W), ('front', 'blk'))  314 us
    another operation x18, other arithmetic, right_solve(): return jax.scipy.linalg.solve_triangular(factor, matrix.T, lower=True).T  290 us
    another operation x55, other arithmetic, blocked_cholesky(): diag_piece = jnp.linalg.cholesky(remaining[offset:finish, offset:finish])  278 us
    all_gather x1, waiting for transfers between devices, shards(): lax.all_gather(child_diag, 'blk', axis=0, tiled=True)  81.6 us
    another operation x63, matrix products, right_solve(): return jax.scipy.linalg.solve_triangular(factor, matrix.T, lower=True).T  61 us
    another operation x86, local copies, waits for them, and re-layouts, right_solve(): return jax.scipy.linalg.solve_triangular(factor, matrix.T, lower=True).T  48.4 us
    another operation x41, local copies, waits for them, and re-layouts  27.3 us
  transfers between devices with their start and end apart: 7, of which 3 were waited for; matrix products, arithmetic and copies ran while one was open for 58% of the time, Pallas kernels for 0%

commit v1 on v0

v1 whole, which is shorter than its diff:
```python
import functools
import jax
import jax.numpy as jnp
from jax import lax
from jax.experimental import pallas as pl
from jax.experimental.pallas import tpu as pltpu
from jax.sharding import PartitionSpec as P

W = 1024
TILE = 128
TA = 4
PB = 4
SUB = 8
HIGHEST=lax.Precision.HIGHEST
NT=(((1,),(1,)),((),()))

def dot_nt(a,b):
    return lax.dot_general(a,b,NT,precision=HIGHEST,preferred_element_type=jnp.float32)

def split(x):
    hi=x.astype(jnp.bfloat16)
    lo=(x-hi.astype(jnp.float32)).astype(jnp.bfloat16)
    return hi,lo

def dot3(ah,al,bh,bl):
    f=lambda p,q: lax.dot_general(p,q,NT,preferred_element_type=jnp.float32)
    return f(ah,bh)+(f(ah,bl)+f(al,bh))

def recip(x):
    r=pl.reciprocal(x,approx=True)
    r=r*(2.0-x*r)
    return r*(2.0-x*r)

def diag_steps(s):
    lane=lax.broadcasted_iota(jnp.int32,(SUB,TILE),1)
    sub=lax.broadcasted_iota(jnp.int32,(SUB,TILE),0)
    full=(SUB,TILE)
    for b in range(TILE//SUB):
        r0=b*SUB
        inside=(lane>=r0)&(lane<r0+SUB)
        v=[jnp.broadcast_to(s[r0+i:r0+i+1,:],full) for i in range(SUB)]
        a=[[jnp.broadcast_to(v[i][:,r0+j:r0+j+1],full) for j in range(i+1)] for i in range(SUB)]
        w=[jnp.where(inside,jnp.where(lane==r0+i,1.0,0.0),v[i]) for i in range(SUB)]
        r=[None]*SUB
        l=[[None]*SUB for _ in range(SUB)]
        for i in range(SUB):
            r[i]=recip(a[i][i])
            for k in range(i+1,SUB):
                l[k][i]=a[k][i]*r[i]
            for k in range(i+1,SUB):
                for m in range(i+1,k+1):
                    a[k][m]=a[k][m]-l[k][i]*a[m][i]
            for k in range(i+1,SUB):
                w[k]=w[k]-l[k][i]*w[i]
        z=[w[i]*r[i] for i in range(SUB)]
        for i in range(SUB-1,0,-1):
            for k in range(i):
                z[k]=z[k]-l[i][k]*z[i]
        for rb in range(b+1,TILE//SUB):
            x=s[rb*SUB:(rb+1)*SUB,:]
            c=[jnp.broadcast_to(x[:,r0+i:r0+i+1],full) for i in range(SUB)]
            p=c[0]*z[0]
            q=c[1]*z[1]
            for i in range(2,SUB,2):
                p=p+c[i]*z[i]
                q=q+c[i+1]*z[i+1]
            s[rb*SUB:(rb+1)*SUB,:]=jnp.where(inside,0.0,x)-(p+q)
        o=w[0]*lax.rsqrt(a[0][0])
        for i in range(1,SUB):
            o=jnp.where(sub==i,w[i]*lax.rsqrt(a[i][i]),o)
        s[r0:r0+SUB,:]=jnp.where(lane<r0+SUB,o,0.0)
        yield b

def diag(s):
    for _ in diag_steps(s): pass


def block(start,size=TILE):
    return pl.ds(pl.multiple_of(start,TILE),size)

def chol_solve(m,x,n,s,inv_hi,inv_lo,p_hi,p_lo,low=None,chunk=256):
    s[...]=m[0:TILE,0:TILE]
    if low is not None:
        low[...]=jnp.zeros((W,W),jnp.float32)
        low[0:TILE,0:TILE]=m[0:TILE,0:TILE]
    diag(s)
    rows=lax.broadcasted_iota(jnp.int32,(chunk,TILE),0)
    def step(j,carry):
        c0=j*TILE; c1=c0+TILE
        inv=s[...]
        ih,il=split(inv)
        inv_hi[...]=ih; inv_lo[...]=il
        if low is not None:
            low[block(c0),block(c0)]=dot_nt(low[block(c0),block(c0)],inv)
        p=dot_nt(m[block(c1),block(c0)],inv)
        new=m[block(c1),block(c1)]-dot_nt(p,p)
        s[...]=new
        if low is not None:
            low[block(c1),block(c1)]=new
        def panel(k):
            r=slice(k*chunk,(k+1)*chunk)
            a,b=split(m[r,block(c0)])
            q=dot3(a,b,inv_hi[...],inv_lo[...])
            q=jnp.where(rows+k*chunk>=c1,q,0.0)
            a,b=split(q)
            p_hi[r,:]=a; p_lo[r,:]=b
            if low is not None:
                low[r,block(c0)]=low[r,block(c0)]+q
        def trail(k):
            r=slice(k*chunk,(k+1)*chunk)
            m[r,:]=m[r,:]-dot3(p_hi[r,:],p_lo[r,:],p_hi[...],p_lo[...])
        def other(k,size):
            r=slice(k*size,(k+1)*size)
            a,b=split(x[r,block(c0)])
            q=dot3(a,b,inv_hi[...],inv_lo[...])
            a,b=split(q)
            x[r,:]=x[r,:]-dot3(a,b,p_hi[...],p_lo[...])
            x[r,block(c0)]=q
        size=min(chunk,n)
        work=[functools.partial(panel,k) for k in range(W//chunk)]
        work+=[functools.partial(trail,k) for k in range(W//chunk)]
        work+=[functools.partial(other,k,size) for k in range(n//size)]
        steps=TILE//SUB
        done=0
        for b in diag_steps(s):
            upto=(b+1)*len(work)//steps
            for f in work[done:upto]: f()
            done=upto
        return carry
    lax.fori_loop(0,W//TILE-1,step,0)
    c0=W-TILE
    inv=s[...]
    a,b=split(inv)
    inv_hi[...]=a; inv_lo[...]=b
    if low is not None:
        low[c0:,c0:]=dot_nt(low[c0:,c0:],inv)
    size=min(chunk,n)
    for k in range(n//size):
        r=slice(k*size,(k+1)*size)
        a,b=split(x[r,c0:])
        x[r,c0:]=dot3(a,b,inv_hi[...],inv_lo[...])

def scratch():
    b=jnp.bfloat16
    return [pltpu.VMEM((TILE,TILE),jnp.float32),pltpu.VMEM((TILE,TILE),b),pltpu.VMEM((TILE,TILE),b),
            pltpu.VMEM((W,TILE),b),pltpu.VMEM((W,TILE),b)]

HBM=pl.BlockSpec(memory_space=pl.ANY)
VM=pl.BlockSpec(memory_space=pltpu.VMEM)

def child_kernel(a_ref,top_ref,rows_ref,schur_ref,cross_ref,m,x,th,tl,sems,*rest):
    T=top_ref.shape[0]; n=T+rows_ref.shape[0]
    cp=[pltpu.make_async_copy(a_ref,m,sems.at[0]),pltpu.make_async_copy(top_ref,x.at[0:T],sems.at[1]),
        pltpu.make_async_copy(rows_ref,x.at[T:n],sems.at[2])]
    for c in cp: c.start()
    for c in cp: c.wait()
    chol_solve(m,x,n,*rest)
    for k in range(T//TILE):
        r=slice(k*TILE,(k+1)*TILE)
        a,b=split(x[r,:]); th[r,:]=a; tl[r,:]=b
    me=lax.axis_index("blk")
    cross_ref[...]=dot_nt(x[pl.ds(pl.multiple_of(me*TILE,TILE),TILE),:],x[0:T,:])
    for k in range((n-T)//TILE):
        r=slice(k*TILE,(k+1)*TILE)
        a,b=split(x[T+k*TILE:T+(k+1)*TILE,:])
        y=dot3(a,b,th[...],tl[...])
        for q in range(T//TILE):
            schur_ref[q,r,:]=y[:,q*TILE:(q+1)*TILE]

def child(a,top,rows):
    T=top.shape[0]; n=T+rows.shape[0]
    return pl.pallas_call(child_kernel,
        out_shape=(jax.ShapeDtypeStruct((T//TILE,rows.shape[0],TILE),jnp.float32),jax.ShapeDtypeStruct((TILE,T),jnp.float32)),
        in_specs=[HBM]*3,out_specs=(VM,VM),
        scratch_shapes=[pltpu.VMEM((W,W),jnp.float32),pltpu.VMEM((n,W),jnp.float32),
          pltpu.VMEM((T,W),jnp.bfloat16),pltpu.VMEM((T,W),jnp.bfloat16),pltpu.SemaphoreType.DMA((3,))]+scratch(),
        compiler_params=pltpu.CompilerParams(vmem_limit_bytes=56*2**20),name="child",
        cost_estimate=pl.CostEstimate(flops=6*2**30,bytes_accessed=2**24,transcendentals=0))(a,top,rows)

def parent_kernel(a_ref,low_ref,inv_ref,m,sem,*rest):
    c=pltpu.make_async_copy(a_ref,m,sem); c.start(); c.wait()
    inv_ref[...]=jnp.where(lax.broadcasted_iota(jnp.int32,(W,W),0)==lax.broadcasted_iota(jnp.int32,(W,W),1),1.0,0.0)
    chol_solve(m,inv_ref,W,*rest,low=low_ref)

def parent(a):
    return pl.pallas_call(parent_kernel,
        out_shape=(jax.ShapeDtypeStruct((W,W),jnp.float32),)*2,
        in_specs=[HBM],out_specs=(VM,VM),
        scratch_shapes=[pltpu.VMEM((W,W),jnp.float32),pltpu.SemaphoreType.DMA]+scratch(),
        compiler_params=pltpu.CompilerParams(vmem_limit_bytes=56*2**20),name="parent",
        cost_estimate=pl.CostEstimate(flops=6*2**30,bytes_accessed=2**24,transcendentals=0))(a)

def place_kernel(position,tiles,out,sems):
    copies=[pltpu.make_async_copy(tiles.at[i],out.at[position[i]],sems.at[i]) for i in range(tiles.shape[0])]
    for c in copies: c.start()
    for c in copies: c.wait()

def place(position,tiles,slots):
    return pl.pallas_call(place_kernel,
        out_shape=jax.ShapeDtypeStruct((slots,TILE,TILE),jnp.float32),
        in_specs=[pl.BlockSpec(memory_space=pltpu.SMEM),HBM],out_specs=HBM,
        scratch_shapes=[pltpu.SemaphoreType.DMA((tiles.shape[0],))],name="place")(position,tiles)

def subtract_kernel(per_step,labels,received,rows,out):
    t=pl.program_id(0)
    @pl.when(t==0)
    def _():
        for p in range(PB):
            out[p]=rows[p*TILE:(p+1)*TILE,:]
    def one(i,carry):
        label=labels[t*per_step+i]
        @pl.when(label>=0)
        def _():
            slot=label//2
            columns=pl.ds(pl.multiple_of((label-slot*2)*TILE,TILE),TILE)
            out[slot,:,columns]=out[slot,:,columns]-received[i]
        return carry
    lax.fori_loop(0,per_step,one,0)

def subtract(labels,received,rows,per_step=16):
    slots=received.shape[0]; width=rows.shape[1]
    return pl.pallas_call(functools.partial(subtract_kernel,per_step),
        out_shape=jax.ShapeDtypeStruct((PB,TILE,width),jnp.float32),
        grid_spec=pltpu.PrefetchScalarGridSpec(num_scalar_prefetch=1,grid=(slots//per_step,),
            in_specs=[pl.BlockSpec((per_step,TILE,TILE),lambda t,lab:(t,0,0)),
                      pl.BlockSpec((PB*TILE,width),lambda t,lab:(0,0))],
            out_specs=pl.BlockSpec((PB,TILE,width),lambda t,lab:(0,0,0))),
        name="subtract")(labels,received,rows)

def sum_parent(cross,row_pick,column_picks,parent_diag,fronts,blocks):
    height=parent_diag.shape[0]
    picked=lambda pick: jnp.stack([jnp.where(pick==0,1.0,0.0),jnp.where(pick==1,1.0,0.0)]).astype(jnp.float32)
    spread=cross.reshape(1,TILE,blocks,1,TILE)*picked(row_pick).reshape(2,1,1,1,1)*picked(column_picks).T.reshape(1,1,blocks,2,1)
    pieces=spread.reshape(fronts,height//fronts,W)
    mine=lax.all_to_all(pieces,"front",split_axis=0,concat_axis=0,tiled=True).sum(0)
    me=lax.axis_index("front")
    part=lax.dynamic_slice_in_dim(parent_diag,me*(height//fronts),height//fronts,0)-mine
    quarter=lax.all_to_all(jnp.broadcast_to(part[None],(fronts,)+part.shape),"front",split_axis=0,concat_axis=0,tiled=True)
    quarter=quarter.reshape(height,W)
    return lax.all_to_all(jnp.broadcast_to(quarter[None],(blocks,)+quarter.shape),"blk",split_axis=0,concat_axis=0,tiled=True).reshape(W,W)

def shards(child_diag,child_top,child_rows,row_owner,row_slot,col_block,parent_diag,parent_rows):
    blocks=lax.axis_size("blk"); fronts=lax.axis_size("front")
    my_block=lax.axis_index("blk")
    quarter=W//(TILE*blocks)
    capacity=2
    owners=row_owner[0,:,0]
    column_picks=col_block[0]
    block_ids=jnp.arange(blocks,dtype=jnp.int32)
    my_pick=jnp.sum(jnp.where(block_ids==my_block,column_picks,0))
    sequence=jnp.arange(owners.shape[0],dtype=jnp.int32)
    earlier=(owners[:,None]==owners[None,:])&(sequence[None,:]<sequence[:,None])
    position=owners*capacity+jnp.sum(earlier.astype(jnp.int32),axis=1)
    landing=row_slot[0]*quarter+my_pick
    hits=position[None,:]==jnp.arange(fronts*capacity,dtype=jnp.int32)[:,None]
    labels=jnp.max(jnp.where(hits,landing[None,:],-1),axis=1)
    labels=lax.all_to_all(labels.reshape(fronts,capacity),"front",split_axis=0,concat_axis=0,tiled=True).reshape(-1)
    diag_whole=lax.all_gather(child_diag,"blk",axis=0,tiled=True)
    top_whole=lax.all_gather(child_top,"blk",axis=0,tiled=True)
    schur,cross=child(diag_whole,top_whole,child_rows)
    arrived=lax.all_to_all(schur,"blk",split_axis=0,concat_axis=0,tiled=True).reshape(blocks*TA,TILE,TILE)
    outgoing=place(position,arrived,fronts*capacity)
    received=lax.all_to_all(outgoing.reshape(fronts,capacity,TILE,TILE),"front",split_axis=0,concat_axis=0,tiled=True)
    whole=sum_parent(cross,my_pick,column_picks,parent_diag,fronts,blocks)
    factor,inverse=parent(whole)
    updated=subtract(labels,received.reshape(-1,TILE,TILE),parent_rows)
    row_major=lax.all_to_all(updated,"blk",split_axis=0,concat_axis=2,tiled=True)
    row_major=row_major.reshape(TILE,W)
    height=parent_diag.shape[0]
    own=lax.dynamic_slice_in_dim(factor,my_block*height,height,0)
    panel=jnp.dot(row_major,inverse,precision=HIGHEST)
    return own,panel


def solution(mesh):
    return jax.shard_map(shards,mesh=mesh,
        in_specs=(P(("front","blk"),None),P(("front","blk"),None),P(("front","blk"),None),P("front",None,None),
                  P("front",None),P("front",None),P("blk",None),P("front","blk")),
        out_specs=(P("blk",None),P(("front","blk"),None)),check_vma=False)
```

time: 1300 us -> 630 us (0.48)
  other arithmetic: 605 us -> 7.08 us
  Pallas kernels: 0 us -> 176 us
  local copies, waits for them, and re-layouts: 128 us -> 11.1 us
  waiting for transfers between devices: 412 us -> 331 us
  matrix products: 85.6 us -> 5.38 us
  blocking collectives: 0 us -> 31.5 us
    another operation x73 -> x1, other arithmetic: 567 us -> 0.07 us  [sum_parent(): jnp.stack([jnp.where(pick == 0, 1.0, 0.0), jnp.where(pick == 1, 1.0, 0.0)])]
    psum x1 -> x0, waiting for transfers between devices: 314 us -> none  [shards(): whole_diag = lax.psum(placed - spread.reshape(W, W), ('front', 'blk'))]
    all_to_all x4 -> x6, waiting for transfers between devices: 16 us -> 209 us  [the longest x1 102 us: shards(): lax.all_to_all(outgoing.reshape(fronts, capacity, TILE, TILE), 'front', s...]
    pallas_call x0 -> x4, Pallas kernels: none -> 176 us  [the longest x1 69.5 us: child(): pl.pallas_call(child_kernel, out_shape=(jax.ShapeDtypeStruct((T // TILE,...]
    another operation x163 -> x0, local copies, waits for them, and re-layouts: 77.5 us -> none  [the longest x86 48.4 us: right_solve(): return jax.scipy.linalg.solve_triangular(factor, matrix.T, lower=True).T]
    another operation x79 -> x0, matrix products: 67.3 us -> none  [the longest x63 61 us: right_solve(): return jax.scipy.linalg.solve_triangular(factor, matrix.T, lower=True).T]
    all_gather x2, waiting for transfers between devices: 81.7 us -> 120 us  [the longest x1 81.9 us: shards(): diag_whole = lax.all_gather(child_diag, 'blk', axis=0, tiled=True)]
    all_to_all x0 -> x1, blocking collectives: none -> 31.5 us  [sum_parent(): lax.all_to_all(pieces, 'front', split_axis=0, concat_axis=0, tiled=True)]
  transfers between devices with their start and end apart: 7 -> 8, of which waited for: 3 -> 5; matrix products, arithmetic and copies ran while one was open for 58% -> 2% of each run, Pallas kernels for 0% -> 28%
where the time goes in v1:
time: 630 us; the launch traced here: 620 us
  waiting for transfers between devices  331 us (53%)
  Pallas kernels  176 us (28%)
  starting transfers between devices  42.1 us (7%)
  blocking collectives  31.5 us (5%)
  between operations  15.5 us (2%)
  local copies, waits for them, and re-layouts  11.1 us (2%)
  other arithmetic  7.08 us (1%)
    all_to_all x1, waiting for transfers between devices, shards(): lax.all_to_all(outgoing.reshape(fronts, capacity, TILE, TILE), 'front', s...  102 us
    all_to_all x1, waiting for transfers between devices, sum_parent(): lax.all_to_all(jnp.broadcast_to(quarter[None], (blocks,) + quarter.shape)...  82.4 us
    all_gather x1, waiting for transfers between devices, shards(): diag_whole = lax.all_gather(child_diag, 'blk', axis=0, tiled=True)  81.9 us
    pallas_call x1, Pallas kernels, child(): pl.pallas_call(child_kernel, out_shape=(jax.ShapeDtypeStruct((T // TILE,...  69.5 us
    pallas_call x1, Pallas kernels, parent(): pl.pallas_call(parent_kernel, out_shape=(jax.ShapeDtypeStruct((W, W), jnp...  65.6 us
    all_gather x1, waiting for transfers between devices, shards(): top_whole = lax.all_gather(child_top, 'blk', axis=0, tiled=True)  38.2 us
    pallas_call x1, Pallas kernels, place(): pl.pallas_call(place_kernel, out_shape=jax.ShapeDtypeStruct((slots, TILE,...  33.7 us
    all_to_all x1, blocking collectives, sum_parent(): lax.all_to_all(pieces, 'front', split_axis=0, concat_axis=0, tiled=True)  31.5 us
  transfers between devices with their start and end apart: 8, of which 5 were waited for; matrix products, arithmetic and copies ran while one was open for 2% of the time, Pallas kernels for 28%

profile of v1, /device:TPU:2, one launch (start us, length us, event | category | flops | bytes accessed | tf_op | source)
XLA Modules:
  0.0 619.7 jit_solution(13720088867157806017)
XLA Ops:
  7.2 0.0 all-gather.5.cloned.1.call-start
  7.2 0.7 all-gather.5.cloned.1.call-update
  7.9 0.0 all-gather.3.cloned.1.call-start
  7.9 0.7 all-gather.3.cloned.1.call-update
  8.7 1.3 fusion.1
  9.9 0.9 convert_reduce_fusion
  10.9 1.3 add_bitcast_fusion
  12.2 0.7 multiply_add_fusion.position
  12.8 0.0 copy-start.1
  12.8 0.1 select_reduce_fusion
  12.9 0.8 all_to_all.35
  13.7 9.4 %all-to-all-start.3 = ((s32[64,1,2]{2,1,0:T(1,128)}), s32[64,1,2]{2,1,0:T(1,128)S(1)}, u32[]{:S(2)}, u32[]{:S(2)}) async-start(s32[64,1,2]{2,1,0:T(1,128)} %bitcast.8), calls=%async_computation.3 | async-start | bytes 65536 | tf_op jit(solution)/shard_map/all_to_all | solution.py:257
  24.4 0.7 compare_select_fusion.1
  25.0 0.1 copy.19
  25.1 0.1 pad_maximum_fusion
  25.2 38.2 %all-gather.5.cloned.1.call-done.top_ref = f32[512,1024]{1,0:T(8,128)} async-done(((f32[128,1024]{1,0:T(8,128)}), f32[512,1024]{1,0:T(8,128)}) %all-gather.5.cloned.1.call-update) | async-done | bytes 2097168 | tf_op jit(solution)/shard_map/all_gather | solution.py:259
  63.4 81.9 %all-gather.3.cloned.1.call-done.a_ref = f32[1024,1024]{1,0:T(8,128)} async-done(((f32[256,1024]{1,0:T(8,128)}), f32[1024,1024]{1,0:T(8,128)}) %all-gather.3.cloned.1.call-update) | async-done | bytes 4194320 | tf_op jit(solution)/shard_map/all_gather | solution.py:258
  145.3 69.5 %child.1 = (f32[4,512,128]{2,1,0:T(8,128)}, f32[128,512]{1,0:T(8,128)}) custom-call(f32[1024,1024]{1,0:T(8,128)} %all-gather.3.cloned.1.call-done.a_ref, f32[512,1024]{1,0:T(8,128)} %all-gather.5.cloned.1.call-done.top_ref, f32[512,1024]{1,0:T(8,128)} %rows_ref.1), custom_call_target="tpu_custom_call" | custom-call | flops 6442450944 | bytes 16777216 | tf_op jit(solution)/shard_map/child/pallas_call | solution.py:172
  214.8 0.0 copy-done.1
  214.9 1.0 mul.58
  215.9 0.1 broadcast_multiply_fusion.1
  216.0 0.4 mul.62
  216.4 1.0 mul.63
  217.4 0.1 mul.64
  217.5 0.2 broadcast_multiply_fusion
  217.8 0.0 all-to-all-done.3
  217.8 31.5 %all_to_all.49 = f32[64,4,1024]{2,1,0:T(4,128)S(1)} all-to-all(f32[64,4,1024]{2,1,0:T(4,128)S(1)} %broadcast_multiply_fusion), channel_id=1, replica_groups=mesh['front'=64,'blk'=4] {'front'}, dimensions={0} | all-to-all | bytes 2097152 | tf_op jit(solution)/shard_map/all_to_all | solution.py:235
  249.2 3.5 all-to-all-start.4
  252.8 0.2 reduce_sum.28
  253.0 0.8 dynamic-slice_subtract_fusion
  253.7 25.2 %all-to-all-done.4 = f32[4,512,128]{2,1,0:T(8,128)S(1)} async-done(((f32[4,512,128]{2,1,0:T(8,128)}), f32[4,512,128]{2,1,0:T(8,128)S(1)}, u32[]{:S(2)}, u32[]{:S(2)}) %all-to-all-start.4) | async-done | bytes 1048608 | tf_op jit(solution)/shard_map/all_to_all | solution.py:261
  278.9 0.0 copy-start
  278.9 1.3 broadcast_in_dim.52
  280.2 7.6 %all-to-all-start.1 = ((f32[64,4,1024]{2,1,0:T(4,128)}), f32[64,4,1024]{2,1,0:T(4,128)S(1)}, u32[]{:S(2)}, u32[]{:S(2)}) async-start(f32[64,4,1024]{2,1,0:T(4,128)} %broadcast_in_dim.52), calls=%async_computation.1 | async-start | bytes 2097152 | tf_op jit(solution)/shard_map/all_to_all | solution.py:238
  287.9 0.0 copy-done
  287.9 33.7 %place.1 = f32[128,128,128]{2,1,0:T(8,128)} custom-call(s32[16]{0:T(128)} %copy-done.1, f32[16,128,128]{2,1,0:T(8,128)} %bitcast.23), custom_call_target="tpu_custom_call" | custom-call | tf_op jit(solution)/shard_map/place/pallas_call | solution.py:199
  321.6 0.0 all-to-all-done.1
  321.6 9.0 %all-to-all-start.5 = ((f32[64,2,128,128]{3,2,1,0:T(8,128)}), f32[64,2,128,128]{3,2,1,0:T(8,128)}, u32[]{:S(2)}, u32[]{:S(2)}) async-start(f32[64,2,128,128]{3,2,1,0:T(8,128)} %bitcast.22), calls=%async_computation.5 | async-start | bytes 16777216 | tf_op jit(solution)/shard_map/all_to_all | solution.py:263
  330.6 0.4 broadcast_in_dim.53
  331.0 101.5 %all-to-all-done.5 = f32[64,2,128,128]{3,2,1,0:T(8,128)} async-done(((f32[64,2,128,128]{3,2,1,0:T(8,128)}), f32[64,2,128,128]{3,2,1,0:T(8,128)}, u32[]{:S(2)}, u32[]{:S(2)}) %all-to-all-start.5) | async-done | bytes 8388640 | tf_op jit(solution)/shard_map/all_to_all | solution.py:263
  432.5 2.5 broadcast_in_dim.54
  435.0 4.9 all-to-all-start.2
  439.9 0.5 broadcast.48
  440.4 0.7 reduce.3
  441.2 0.7 reshape.56.labels
  441.8 7.6 %subtract.1 = f32[4,128,256]{2,1,0:T(8,128)} custom-call(s32[128]{0:T(128)} %reshape.56.labels, f32[128,128,128]{2,1,0:T(8,128)} %bitcast.11.received, f32[512,256]{1,0:T(8,128)} %rows.1), custom_call_target="tpu_custom_call" | custom-call | tf_op jit(solution)/shard_map/subtract/pallas_call | solution.py:222
  449.4 82.4 %all-to-all-done.2 = f32[4,256,1024]{2,1,0:T(8,128)} async-done(((f32[4,256,1024]{2,1,0:T(8,128)}), f32[4,256,1024]{2,1,0:T(8,128)}, u32[]{:S(2)}, u32[]{:S(2)}) %all-to-all-start.2) | async-done | bytes 4194336 | tf_op jit(solution)/shard_map/all_to_all | solution.py:240
  531.8 7.5 %all-to-all-start.6 = ((f32[4,128,256]{2,1,0:T(8,128)}), f32[4,128,256]{2,1,0:T(8,128)S(1)}, u32[]{:S(2)}, u32[]{:S(2)}) async-start(f32[4,128,256]{2,1,0:T(8,128)} %subtract.1), calls=%async_computation.6 | async-start | bytes 1048576 | tf_op jit(solution)/shard_map/all_to_all | solution.py:267
  539.3 65.6 %parent.1 = (f32[1024,1024]{1,0:T(8,128)}, f32[1024,1024]{1,0:T(8,128)}) custom-call(f32[1024,1024]{1,0:T(8,128)} %bitcast.5.a_ref), custom_call_target="tpu_custom_call" | custom-call | flops 6442450944 | bytes 16777216 | tf_op jit(solution)/shard_map/parent/pallas_call | solution.py:186
  604.9 2.3 constant_dynamic-slice_fusion
  607.3 0.0 all-to-all-done.6
  607.3 0.2 copy.22
  607.5 5.4 fusion.2
  (1 shorter events, 0.0 us)
Async XLA Ops:
  7.2 56.3 %all-gather.5.cloned.1.call-start = ((), (), s32[]{:S(2)}) async-start(), calls=%async_computation.8 | async-start | bytes 2621440 | tf_op jit(solution)/shard_map/all_gather | solution.py:259
  7.9 137.4 %all-gather.3.cloned.1.call-start = ((), (), s32[]{:S(2)}) async-start(), calls=%async_computation.7 | async-start | bytes 5242880 | tf_op jit(solution)/shard_map/all_gather | solution.py:258
  12.8 202.0 %copy-start.1 = (s32[16]{0:T(128)}, s32[16]{0:T(128)S(1)}, u32[]{:S(2)}) copy-start(s32[16]{0:T(128)S(1)} %multiply_add_fusion.position) | copy-start | bytes 196
  13.7 204.1 %all-to-all-start.3 = ((s32[64,1,2]{2,1,0:T(1,128)}), s32[64,1,2]{2,1,0:T(1,128)S(1)}, u32[]{:S(2)}, u32[]{:S(2)}) async-start(s32[64,1,2]{2,1,0:T(1,128)} %bitcast.8), calls=%async_computation.3 | async-start | bytes 65536 | tf_op jit(solution)/shard_map/all_to_all | solution.py:257
  249.2 29.7 %all-to-all-start.4 = ((f32[4,512,128]{2,1,0:T(8,128)}), f32[4,512,128]{2,1,0:T(8,128)S(1)}, u32[]{:S(2)}, u32[]{:S(2)}) async-start(f32[4,512,128]{2,1,0:T(8,128)} %get-tuple-element.8), calls=%async_computation.4 | async-start | bytes 2097152 | tf_op jit(solution)/shard_map/all_to_all | solution.py:261
  278.9 9.0 %copy-start = (f32[4,512,128]{2,1,0:T(8,128)}, f32[4,512,128]{2,1,0:T(8,128)S(1)}, u32[]{:S(2)}) copy-start(f32[4,512,128]{2,1,0:T(8,128)S(1)} %all-to-all-done.4) | copy-start | bytes 3145732
  280.2 41.3 %all-to-all-start.1 = ((f32[64,4,1024]{2,1,0:T(4,128)}), f32[64,4,1024]{2,1,0:T(4,128)S(1)}, u32[]{:S(2)}, u32[]{:S(2)}) async-start(f32[64,4,1024]{2,1,0:T(4,128)} %broadcast_in_dim.52), calls=%async_computation.1 | async-start | bytes 2097152 | tf_op jit(solution)/shard_map/all_to_all | solution.py:238
  321.6 111.0 %all-to-all-start.5 = ((f32[64,2,128,128]{3,2,1,0:T(8,128)}), f32[64,2,128,128]{3,2,1,0:T(8,128)}, u32[]{:S(2)}, u32[]{:S(2)}) async-start(f32[64,2,128,128]{3,2,1,0:T(8,128)} %bitcast.22), calls=%async_computation.5 | async-start | bytes 16777216 | tf_op jit(solution)/shard_map/all_to_all | solution.py:263
  435.0 96.8 %all-to-all-start.2 = ((f32[4,256,1024]{2,1,0:T(8,128)}), f32[4,256,1024]{2,1,0:T(8,128)}, u32[]{:S(2)}, u32[]{:S(2)}) async-start(f32[4,256,1024]{2,1,0:T(8,128)} %broadcast_in_dim.54), calls=%async_computation.2 | async-start | bytes 8388608 | tf_op jit(solution)/shard_map/all_to_all | solution.py:240
  531.8 75.4 %all-to-all-start.6 = ((f32[4,128,256]{2,1,0:T(8,128)}), f32[4,128,256]{2,1,0:T(8,128)S(1)}, u32[]{:S(2)}, u32[]{:S(2)}) async-start(f32[4,128,256]{2,1,0:T(8,128)} %subtract.1), calls=%async_computation.6 | async-start | bytes 1048576 | tf_op jit(solution)/shard_map/all_to_all | solution.py:267
Sparse Core Ops, SparseCore 0:
  9.8 53.5 all-gather.4
  65.2 80.0 all-gather.2
